TPU v7x, 32 devices: a whole 2x2x4 slice. The times are simulated.
32 devices in a mesh: dp: 16 (over z, y, x), tensor: 2 (over core).
Axes of the slice: x: 2, y: 2, z: 4, core: 2. Of those that a mesh axis runs over, the one named last changes fastest.
Arguments:
- tokens: bfloat16 [16384, 768], P(('dp', 'tensor')), may hold values from -6 to 6
- qkv_weight: bfloat16 [768, 3, 768], P(None, None, 'tensor'), may hold values from -0.21875 to 0.21875
- qv_bias: float32 [2, 768], P(None, 'tensor'), may hold values from -3 to 3
- rel_table: float32 [256, 12], P(None, 'tensor'), may hold values from -4 to 4
- out_weight: bfloat16 [768, 768], P('tensor'), may hold values from -1.25 to 1.25
- out_bias: float32 [768], replicated, may hold values from -3 to 3
- norm1_gain: float32 [768], replicated, may hold values from 0.5 to 1.5
- norm1_bias: float32 [768], replicated, may hold values from -3 to 3
- up_weight: bfloat16 [768, 3072], P(None, 'tensor'), may hold values from -0.21875 to 0.21875
- up_bias: float32 [3072], P('tensor'), may hold values from -3 to 3
- down_weight: bfloat16 [3072, 768], P('tensor'), may hold values from -0.109375 to 0.109375
- down_bias: float32 [768], replicated, may hold values from -3 to 3
- norm2_gain: float32 [768], replicated, may hold values from 0.5 to 1.5
- norm2_bias: float32 [768], replicated, may hold values from -3 to 3
- rel_bucket: int32 [512, 512], replicated, may hold values from 0 to 127
- query_len: int32 [32], P('dp'), may hold values from 1 to 128
- key_mask: int32 [32, 512], P('dp'), may hold values from 0 to 1, as said below
- upstream: bfloat16 [16384, 768], P(('dp', 'tensor')), may hold values from -6 to 6
Outputs:
- out: bfloat16 [16384, 768], P(('dp', 'tensor'))
- grad_tokens: float32 [16384, 768], P(('dp', 'tensor'))
- grad_qkv_weight: float32 [768, 3, 768], P(None, None, 'tensor')
- grad_qv_bias: float32 [2, 768], P(None, 'tensor')
- grad_rel_table: float32 [256, 12], P(None, 'tensor')
- grad_out_weight: float32 [768, 768], P('tensor')
- grad_out_bias: float32 [768], replicated
- grad_norm1_gain: float32 [768], replicated
- grad_norm1_bias: float32 [768], replicated
- grad_up_weight: float32 [768, 3072], P(None, 'tensor')
- grad_up_bias: float32 [3072], P('tensor')
- grad_down_weight: float32 [3072, 768], P('tensor')
- grad_down_bias: float32 [768], replicated
- grad_norm2_gain: float32 [768], replicated
- grad_norm2_bias: float32 [768], replicated
Inputs may be any that keep to these rules, and one draw needn't show every extreme that they name: Each row of key_mask is 1 on its first positions and 0 after them, with 256 or more ones; in every draw some pair has no padding.
All inputs are finite; a program needn't handle non-finite values.
Results may differ from a plain program's by a relative error of at most 0.017.
The roundings to bfloat16 on the way count: a program that leaves them out, or rounds other values in their place, can miss the bound.
Values may be sent and summed in bfloat16 or wider, within the bound.
A program may use at most 192 MiB of HBM per device.

v0:
```python
import functools
import math

import jax
import jax.numpy as jnp
from jax import lax
from jax.experimental import pallas as pl
from jax.experimental.pallas import tpu as pltpu
from jax.sharding import PartitionSpec as P

EPSILON = 1e-05
FAR_BELOW = -1000000000.0
MESH = pl.DeviceIdType.MESH
F32 = jnp.float32
BF16 = jnp.bfloat16
LANES = 128
NT = (((1,), (1,)), ((), ()))
TN = (((0,), (0,)), ((), ()))
VMEM_LIMIT = 62 * 2**20
ORDERS = {
    "down": ((2, "xyD", "yxD"), (3, "yxzZ", "zZxy"), (1, "xyzZ", "xzZy")),
    "up": ((2, "xyzZ", "xyzZ"), (1, "xyzZ", "zZxy"), (1, "yxzZ", "yzZx")),
    "out": ("xyzZ", "yxzZ"),
    "mix": (("xyD", "yxD"), ("yxD", "yxD"), ("yxD", "xyD")),
}
PAUSES = {
    12: ((0, 1),),
    15: ((2, 1),),
    16: ((1, 1),),
    18: ((0, 2),),
    19: ((5, 1),),
    20: ((2, 2),),
    22: ((3, 1), (0, 3), (4, 1), (2, 3)),
    24: ((1, 2),),
    25: ((6, 1), (0, 4), (3, 2), (2, 4)),
    26: ((5, 2),),
    27: ((1, 3),),
    28: ((4, 2),),
    29: ((6, 2),),
    31: ((3, 3),),
    32: ((2, 5), (0, 5)),
    33: ((5, 3),),
    35: ((1, 4), (4, 3)),
    36: ((6, 3),),
    37: ((7, 1), (3, 4), (2, 6)),
    39: ((5, 4),),
    42: ((6, 4), (8, 1)),
    43: ((9, 1), (3, 5)),
    44: ((5, 5),),
    45: ((7, 2), (6, 5)),
    46: ((8, 2), (2, 7)),
    47: ((1, 5), (0, 6), (3, 6), (4, 4)),
    48: ((5, 6), (10, 1), (9, 2)),
    50: ((7, 3), (6, 6), (2, 8)),
}
TAIL = ((8, 3), (3, 7), (10, 2), (4, 5), (1, 6), (5, 7), (10, 3), (6, 7), (9, 3), (7, 4), (8, 4), (5, 8), (4, 6), (3, 8), (7, 5), (10, 4), (1, 7), (9, 4), (6, 8), (4, 7), (8, 5), (10, 5), (7, 6), (9, 5), (1, 8), (8, 6), (4, 8), (9, 6))


def dot(left, right, dims=None):
    if dims is None:
        return jnp.dot(left, right, preferred_element_type=F32)
    return lax.dot_general(left, right, dims, preferred_element_type=F32)


def other_core():
    return {"tensor": 1 - lax.axis_index("tensor")}


def row(ref):
    return ref[...].reshape(1, ref.shape[-1])


def fold8(block):
    return jnp.sum(block.reshape(block.shape[0] // 8, 8, block.shape[1]), axis=0)


def pack_tables(tab, packed, core):
    step = jnp.maximum(jnp.max(jnp.abs(tab[core])), 1e-30) / 32000.0
    inverse = 1.0 / step
    heads = tab.shape[1]
    for pair in range(heads // 2):
        high = tab[core, 2 * pair : 2 * pair + 1, :] * inverse
        low = jnp.round(tab[core, 2 * pair + 1 : 2 * pair + 2, :] * inverse)
        high = jnp.round(high - low * (1 / 65536.0))
        both = high.astype(jnp.int32) * 65536 + low.astype(jnp.int32)
        packed[core * (heads // 2) + pair] = jnp.broadcast_to(both, packed.shape[1:])
    return step


def attend_pair(pair, q, k, vt, packed, bucket, valid, length, step, expo, heads_t, recip):
    seq = q.shape[0]
    cols = pl.ds(pl.multiple_of(pair * LANES, LANES), LANES)
    keys = k[:, cols]
    queries = q[:, cols]
    lane = lax.broadcasted_iota(jnp.int32, (seq, LANES), 1)
    in_query = lax.broadcasted_iota(jnp.int32, (seq, LANES), 0) < length
    terms = packed[pair, 0:1, :]
    near = jnp.broadcast_to(terms[:, :LANES], (seq, LANES))
    far = jnp.broadcast_to(terms[:, LANES:], (seq, LANES))
    same = jnp.where(in_query, far, near)
    swap = jnp.where(in_query, near, far)
    pieces = ([], [])
    for start in range(0, seq, LANES):
        index = bucket[:, start : start + LANES]
        got = jnp.take_along_axis(same, index, axis=1, mode="promise_in_bounds")
        if start == 0:
            turned = jnp.take_along_axis(swap, index, axis=1, mode="promise_in_bounds")
            got = jnp.where(lane < length, turned, got)
        pieces[0].append(got.astype(F32) * (step * (1 / 65536.0)))
        pieces[1].append(jnp.left_shift(got, 16).astype(F32) * (step * (1 / 65536.0)))
    first = lane < LANES // 2
    real = jnp.concatenate([valid[...] > 0] * (seq // LANES), axis=1)
    for side in range(2):
        mine = first if side == 0 else jnp.logical_not(first)
        scores = dot(jnp.where(mine, keys, jnp.zeros_like(keys)), queries, NT)
        scores = scores + jnp.concatenate(pieces[side], axis=1)
        scores = jnp.where(real, scores, FAR_BELOW)
        highest = jnp.max(scores, axis=0, keepdims=True)
        weights = jnp.exp(scores - highest).astype(BF16)
        expo[2 * pair + side] = weights
        rows = pl.ds(pl.multiple_of(pair * LANES + side * 64, 64), 64)
        values = jnp.concatenate([vt[rows, :], jnp.ones((16, seq), BF16)], axis=0)
        got = dot(values, weights)
        inverse = 1.0 / got[64:65]
        heads_t[rows, :] = (got[:64] * inverse).astype(BF16)
        recip[2 * pair + side] = jnp.broadcast_to(inverse, recip.shape[1:])


def dp_stride(bits):
    first, second = 1 << bits[0], 1 << bits[1]
    if first == second:
        return first
    return first + lax.axis_index("tensor") * (second - first)


def dp_side(bits):
    return lax.rem(lax.div(lax.axis_index("dp"), dp_stride(bits)), 2)


def dp_partner(bits):
    return {"dp": lax.axis_index("dp") + (1 - 2 * dp_side(bits)) * dp_stride(bits)}


def dp_quarter(ahead):
    return lax.rem(lax.div(lax.axis_index("dp"), 4) + ahead, 4)


def dp_ahead(ahead):
    return {"dp": lax.axis_index("dp") + 4 * (dp_quarter(ahead) - dp_quarter(0))}


def flat_rows(start, size):
    return pl.ds(pl.multiple_of(start, 16), size)


class Kit:
    def __init__(self, acc, landing, result, send_sem, recv_sem, local_sem):
        self.acc, self.landing, self.result = acc, landing, result
        self.send_sem, self.recv_sem, self.local_sem = send_sem, recv_sem, local_sem
        self.used = [0, 0]
        self.landed = 0
        self.pieces = []

    def slot(self, kind):
        self.used[kind] += 1
        return self.used[kind] - 1

    def room(self, size):
        self.landed += size
        return self.landed - size

    def remote(self, slot, source, target, device):
        return pltpu.make_async_remote_copy(
            src_ref=source,
            dst_ref=target,
            send_sem=self.send_sem.at[slot[0]],
            recv_sem=self.recv_sem.at[slot[1]],
            device_id=device,
            device_id_type=MESH,
        )


class Piece:
    def __init__(self, start, length, stages, extra, kit):
        self.start = start
        self.stages, self.extra = stages, extra
        self.kit = kit
        self.number = len(kit.pieces)
        self.steps = 2 * len(stages) + 1
        kit.pieces.append(self)
        self.sizes = [length]
        self.cutting, self.spreading = [], []
        for stage in stages:
            parts = 4 if stage is None else 2
            size = self.sizes[-1] // parts
            self.sizes.append(size)
            leaving = [kit.slot(0) for _ in range(parts - 1)]
            self.cutting.append([((slot, kit.slot(1)), kit.room(size)) for slot in leaving])
            self.spreading.append([(slot, kit.slot(1)) for slot in leaving])
        self.crossing = [((kit.slot(0), kit.slot(1)), kit.room(self.sizes[-1])) for _ in extra]

    def begin(self, levels):
        at = self.start
        for level in range(levels):
            stage = self.stages[level]
            at = at + (dp_quarter(0) if stage is None else dp_side(stage)) * self.sizes[level + 1]
        return at

    def partners(self, stage):
        if stage is None:
            return [(dp_quarter(ahead), dp_ahead(ahead)) for ahead in (1, 2, 3)]
        return [(1 - dp_side(stage), dp_partner(stage))]

    def cut(self, level):
        kit, size = self.kit, self.sizes[level + 1]
        at = self.begin(level)
        return [
            kit.remote(
                slot,
                kit.acc.at[flat_rows(at + part * size, size), :],
                kit.landing.at[pl.ds(room, size), :],
                device,
            )
            for (slot, room), (part, device) in zip(
                self.cutting[level], self.partners(self.stages[level])
            )
        ]

    def swap(self, number):
        kit = self.kit
        slot, room = self.crossing[number]
        size = self.sizes[-1]
        return kit.remote(
            slot,
            kit.acc.at[flat_rows(self.begin(len(self.stages)), size), :],
            kit.landing.at[pl.ds(room, size), :],
            dp_partner(self.extra[number]),
        )

    def keep(self):
        kit = self.kit
        mine = flat_rows(self.begin(len(self.stages)), self.sizes[-1])
        return pltpu.make_async_copy(
            kit.acc.at[mine, :], kit.result.at[mine, :], kit.local_sem.at[self.number]
        )

    def spread(self, level):
        kit = self.kit
        mine = flat_rows(self.begin(level + 1), self.sizes[level + 1])
        source = kit.acc if level == len(self.stages) - 1 else kit.result
        return [
            kit.remote(slot, source.at[mine, :], kit.result.at[mine, :], device)
            for slot, (_, device) in zip(
                self.spreading[level], self.partners(self.stages[level])
            )
        ]

    def add(self, target, rooms, size):
        kit = self.kit
        chunk = math.gcd(size, 192)

        def some(number, carry):
            there = flat_rows(target + number * chunk, chunk)
            total = kit.acc[there, :].astype(F32)
            for room in rooms:
                total = total + kit.landing[flat_rows(room + number * chunk, chunk), :].astype(F32)
            kit.acc[there, :] = total.astype(BF16)
            return carry

        lax.fori_loop(0, size // chunk, some, 0)

    def run(self, step):
        levels = len(self.stages)
        if 0 < step <= levels:
            for copy in self.cut(step - 1):
                copy.wait_recv()
            rooms = [room for _, room in self.cutting[step - 1]]
            self.add(self.begin(step), rooms, self.sizes[step])
        if step < levels:
            for copy in self.cut(step):
                copy.start()
            return
        if step == levels:
            for number in range(len(self.extra)):
                both = self.swap(number)
                both.start()
                both.wait()
                self.add(self.begin(levels), [self.crossing[number][1]], self.sizes[-1])
            self.keep().start()
        else:
            for copy in self.spread(2 * levels - step):
                copy.wait_recv()
            if step == levels + 1:
                self.keep().wait()
        if step < 2 * levels:
            for copy in self.cut(2 * levels - 1 - step):
                copy.wait_send()
            for copy in self.spread(2 * levels - 1 - step):
                copy.start()

    def finish(self):
        for level in range(len(self.stages)):
            for copy in self.spread(level):
                copy.wait_send()


class Vectors:
    def __init__(self, parts, landing, result, bits, kit, send_sem, recv_sem):
        self.parts, self.landing, self.result = parts, landing, result
        self.bits = bits
        self.steps = bits + 2
        self.send_sem, self.recv_sem = send_sem, recv_sem
        kit.pieces.append(self)

    def exchange(self, step):
        return pltpu.make_async_remote_copy(
            src_ref=self.parts.at[step],
            dst_ref=self.landing.at[step],
            send_sem=self.send_sem.at[step],
            recv_sem=self.recv_sem.at[step],
            device_id=other_core() if step == 0 else dp_partner((step - 1, step - 1)),
            device_id_type=MESH,
        )

    def run(self, step):
        if step > 0:
            self.exchange(step - 1).wait_recv()
            total = self.parts[max(step - 1, 1)] + self.landing[step - 1]
            if step <= self.bits:
                self.parts[step] = total
            else:
                self.result[...] = total
        if step <= self.bits:
            self.exchange(step).start()

    def finish(self):
        for step in range(self.bits + 1):
            self.exchange(step).wait_send()


def layer_kernel(
    plan,
    bits,
    tokens_h,
    qkvw_h,
    qvb_h,
    tab_h,
    outw_h,
    upw_h,
    upb_h,
    downw_h,
    upstream_h,
    bucket_h,
    outb,
    gain1,
    shift1,
    downb,
    gain2,
    shift2,
    mask,
    length,
    result_h,
    gtok_h,
    out_h,
    small,
    qkvw_o,
    outw_o,
    upw_o,
    downw_o,
    expo_h,
    acc,
    xsend,
    xrecv,
    landing,
    tokens,
    qvb,
    tab,
    upb,
    upb_other,
    upb_rows,
    outw,
    q,
    k,
    v,
    heads_t,
    recip,
    bucket,
    wide,
    gmid16,
    upstream,
    ups,
    vparts,
    vland,
    in_sem,
    out_sem,
    send_sem,
    recv_sem,
    local_sem,
    xs_sem,
    xr_sem,
    vs_sem,
    vr_sem,
    ws_sem,
    wr_sem,
):
    seq, width = tokens.shape
    inner = outw.shape[1]
    units = upw_h.shape[1]
    heads = recip.shape[0]
    pairs = inner // LANES
    split = width // inner
    third = acc.shape[0] // 3

    barrier = pltpu.get_barrier_semaphore()
    pl.semaphore_signal(barrier, inc=1, device_id=other_core(), device_id_type=MESH)
    for bit in range(bits):
        pl.semaphore_signal(barrier, inc=1, device_id=dp_partner((bit, bit)), device_id_type=MESH)
    pl.semaphore_signal(
        barrier,
        inc=1,
        device_id={"dp": lax.axis_index("dp") + 12 - 8 * dp_quarter(0)},
        device_id_type=MESH,
    )

    used, stored = [], []

    def load(source, target):
        copy = pltpu.make_async_copy(source, target, in_sem.at[len(used)])
        used.append(copy)
        copy.start()
        return copy

    loaded = []

    def early(source, target):
        number = len(used)
        used.append(None)
        loaded.append(lambda: pltpu.make_async_copy(source, target(), in_sem.at[number]))
        loaded[-1]().start()

    def store(source, target):
        copy = pltpu.make_async_copy(source, target, out_sem.at[len(stored)])
        stored.append(copy)
        copy.start()
        return copy

    halves = [
        (qkvw_h, qkvw_o),
        (qvb_h, qvb.at[1]),
        (tab_h, tab.at[1]),
        (outw_h, outw_o),
        (upw_h, upw_o),
        (upb_h, upb_other),
        (downw_h, downw_o),
    ]

    def half(number):
        source, target = halves[number]
        return pltpu.make_async_remote_copy(
            src_ref=source,
            dst_ref=target,
            send_sem=ws_sem.at[number],
            recv_sem=wr_sem.at[number],
            device_id=other_core(),
            device_id_type=MESH,
        )

    kit = Kit(acc, landing, result_h, send_sem, recv_sem, local_sem)
    extra = tuple((bit, bit) for bit in range(4, bits))
    crossed = []

    def cross(start, size, place):
        number = len(crossed)

        def copy():
            return pltpu.make_async_remote_copy(
                src_ref=xsend.at[pl.ds(place, size), :],
                dst_ref=xrecv.at[pl.ds(start, size), :],
                send_sem=xs_sem.at[number],
                recv_sem=xr_sem.at[number],
                device_id=other_core(),
                device_id_type=MESH,
            )

        copy().start()
        crossed.append(copy)

    polls = [0]

    def run_steps(number):
        for piece, step in plan.get(number, ()):
            kit.pieces[piece].run(step)

    def poll():
        run_steps(polls[0])
        polls[0] += 1

    def polled_loop(low, high, body, initial, every=1):
        start = polls[0]
        pauses = (high - low) // every
        polls[0] += pauses
        busy = [number for number in range(pauses) if plan.get(start + number)]

        def turn(index, carry):
            carry = body(index, carry)
            for number in busy:

                @pl.when(index == low + (number + 1) * every - 1)
                def _():
                    run_steps(start + number)

            return carry

        return lax.fori_loop(low, high, turn, initial)

    def begin_piece(start, size, orders):
        order = tuple(
            None if one == "D" else ("xyzZ".index(one), "xyzZ".index(two))
            for one, two in zip(*orders)
        )
        fresh = Piece(start, size, order, extra, kit)
        if not any((fresh.number, 0) in steps for steps in plan.values()):
            fresh.run(0)

    def give(place, tile):
        xsend[flat_rows(place, tile.shape[0]), :] = tile.astype(BF16)

    def take(start, tile):
        there = flat_rows(start, tile.shape[0])
        acc[there, :] = (tile + xrecv[there, :].astype(F32)).astype(BF16)

    me = lax.axis_index("tensor")

    def attend_phase(upw, downw, qkvw, vt, bucket_i, bucket_t, valid, packed, expo):
        l_tokens = load(tokens_h, tokens)
        l_qkvw = load(qkvw_h, qkvw.at[0])
        l_qvb = load(qvb_h, qvb.at[0])
        l_bucket = load(bucket_h, bucket_i)
        l_tab = load(tab_h, tab.at[0])
        l_late = [load(outw_h, outw.at[0]), load(upb_h, upb)]
        early(upw_h, lambda: upw.at[0])
        early(downw_h, lambda: downw.at[0])
        early(upstream_h, lambda: upstream)
        span = length[me]
        mine = mask[pl.ds(me, 1), :].astype(F32)
        valid[...] = jnp.transpose(jnp.broadcast_to(mine, (LANES, seq)))

        def mix(core):
            rows = tokens[...]
            cols = slice(core * inner, (core + 1) * inner)
            query = dot(rows, qkvw[core, 0])
            q[:, cols] = ((query + qvb[core, 0:1, :]) * 0.125).astype(BF16)
            k[:, cols] = dot(rows, qkvw[core, 1]).astype(BF16)
            value = (dot(rows, qkvw[core, 2]) + qvb[core, 1:2, :]).astype(BF16)
            v[:, cols] = value
            vt[cols, :] = jnp.transpose(value)

        l_tokens.wait()
        l_qkvw.wait()
        l_qvb.wait()
        mix(0)
        pl.semaphore_wait(barrier, 2 + bits)
        for number in range(3):
            half(number).start()
        l_bucket.wait()
        bucket_t[...] = jnp.transpose(bucket_i[...])
        bucket[...] = bucket_t[...].astype(BF16)
        l_tab.wait()

        def attend(step, pair, carry):
            attend_pair(pair, q, k, vt, packed, bucket_t, valid, span, step, expo, heads_t, recip)
            return carry

        attend_own = functools.partial(attend, pack_tables(tab, packed, 0))

        kept = []

        def keep(low, high):
            here = pl.ds(2 * low, 2 * (high - low))
            kept.append(store(expo.at[here], expo_h.at[here]))

        lax.fori_loop(0, 2, attend_own, 0, unroll=2)
        half(0).wait_recv()
        half(1).wait_recv()
        half(2).wait_recv()
        l_other = load(qkvw_o, qkvw.at[1])
        for number in range(3, 6):
            half(number).start()
        lax.fori_loop(2, pairs, attend_own, 0, unroll=2)
        keep(0, pairs)
        l_other.wait()
        mix(1)
        attend_other = functools.partial(attend, pack_tables(tab, packed, 1))
        lax.fori_loop(pairs, pairs + 1, attend_other, 0)
        keep(pairs, pairs + 1)
        half(6).start()
        half(3).wait_recv()
        l_late.append(load(outw_o, outw.at[1]))
        lax.fori_loop(pairs + 1, 2 * pairs, attend_other, 0, unroll=2)
        keep(pairs + 1, 2 * pairs)
        half(4).wait_recv()
        early(upw_o, lambda: upw.at[1])
        for copy in l_late:
            copy.wait()
        lower = jnp.transpose(heads_t[...])

        def project(tile, carry):
            cols = pl.ds(pl.multiple_of(tile * 256, 256), 256)
            wide[:, cols] = dot(lower[:, :inner], outw[0, :, cols]) + dot(
                lower[:, inner:], outw[1, :, cols]
            )
            return carry

        lax.fori_loop(0, width // 256, project, 0, unroll=3)
        for copy in kept:
            copy.wait()

    def unit_phase(
        upw, downw, act, slope, first, first_t, first32, normed1, inverse1, gsec, gbr, out
    ):
        half(5).wait_recv()
        upb_rows[0] = row(upb)
        upb_rows[1] = row(upb_other)
        block = 128

        def norm_one(number, carry):
            rows = pl.ds(pl.multiple_of(number * block, block), block)
            value = wide[rows, :] + row(outb) + tokens[rows, :].astype(F32)
            center = value - jnp.mean(value, axis=-1, keepdims=True)
            inverse = lax.rsqrt(jnp.mean(center * center, axis=-1, keepdims=True) + EPSILON)
            normed = center * inverse
            result = normed * row(gain1) + row(shift1)
            normed1[rows, :] = normed
            inverse1[rows, :] = jnp.broadcast_to(inverse, (block, LANES))
            first32[rows, :] = result
            first[rows, :] = result.astype(BF16)
            return carry

        lax.fori_loop(0, seq // block, norm_one, 0)

        for core in range(2):
            loaded[3 * core]().wait()

            def expand(tile, carry, core=core):
                cols = pl.ds(pl.multiple_of(tile * 256, 256), 256)
                here = pl.ds(pl.multiple_of(core * units + tile * 256, 256), 256)
                hidden = dot(first[...], upw[core, :, cols]) + upb_rows[core, :, cols]
                chance = 0.5 * (1.0 + lax.erf(hidden * math.sqrt(0.5)))
                density = jnp.exp(hidden * hidden * -0.5) * (1.0 / math.sqrt(2.0 * math.pi))
                act[:, here] = (hidden * chance).astype(BF16)
                slope[:, here] = (chance + hidden * density).astype(BF16)
                return carry

            lax.fori_loop(0, units // 256, expand, 0, unroll=2)
        half(6).wait_recv()
        l_down = load(downw_o, downw.at[1])
        first_t[...] = jnp.transpose(first[...])
        loaded[1]().wait()
        l_down.wait()

        def reduce_units(tile, carry):
            cols = pl.ds(pl.multiple_of(tile * 256, 256), 256)
            wide[:, cols] = dot(act[:, :units], downw[0, :, cols]) + dot(
                act[:, units:], downw[1, :, cols]
            )
            return carry

        lax.fori_loop(0, width // 256, reduce_units, 0, unroll=3)
        loaded[2]().wait()

        def norm_two(number, carry):
            rows = pl.ds(pl.multiple_of(number * block, block), block)
            value = wide[rows, :] + row(downb) + first32[rows, :]
            center = value - jnp.mean(value, axis=-1, keepdims=True)
            inverse = lax.rsqrt(jnp.mean(center * center, axis=-1, keepdims=True) + EPSILON)
            normed = center * inverse
            out[rows, :] = (normed * row(gain2) + row(shift2)).astype(BF16)
            grad = upstream[rows, :].astype(F32)
            scaled = grad * row(gain2)
            back = inverse * (
                scaled
                - jnp.mean(scaled, axis=-1, keepdims=True)
                - normed * jnp.mean(scaled * normed, axis=-1, keepdims=True)
            )
            gsec[rows, :] = back
            gbr[rows, :] = back.astype(BF16)
            return (
                carry[0] + fold8(back),
                carry[1] + fold8(grad * normed),
                carry[2] + fold8(grad),
            )

        zero = jnp.zeros((8, width), F32)
        later = lax.fori_loop(0, seq // block, norm_two, (zero, zero, zero))
        kept = store(out, out_h)

        tiles = units // 256
        span = 256 * split

        def down(core):
            low = 0
            for part, (count, *order) in enumerate(ORDERS["down"]):
                if core == 0:
                    crossed[part]().wait_recv()

                def down_tile(number, carry, core=core):
                    cols = pl.ds(pl.multiple_of(core * units + number * 256, 256), 256)
                    tile = dot(act[:, cols], gbr[...], TN)
                    for side in range(split):
                        (give if core == 1 else take)(
                            number * span + side * 256,
                            tile[:, side * inner : (side + 1) * inner],
                        )
                    return carry

                lax.fori_loop(low, low + count, down_tile, 0)
                if core == 1:
                    cross(low * span, count * span, low * span)
                else:
                    begin_piece(low * span, count * span, order)
                    poll()
                low += count

        def bend(core):
            def slope_tile(number, carry):
                here = pl.ds(pl.multiple_of(number * 256, 256), 256)
                cols = pl.ds(pl.multiple_of(core * units + number * 256, 256), 256)
                tile = dot(gbr[...], downw[core, here, :], NT) * slope[:, cols].astype(F32)
                tile = tile.astype(BF16)
                slope[:, cols] = tile
                ups[core, :, here] = fold8(tile.astype(F32))
                return carry

            polled_loop(0, tiles, slope_tile, 0, tiles // 2)

        down(1)
        fed = len(crossed)
        bend(1)
        down(0)
        bend(0)

        for copy in crossed[:fed]:
            copy().wait_send()
        def up(core):
            low = 0
            for part, (count, *order) in enumerate(ORDERS["up"]):
                if core == 0:
                    crossed[fed + part]().wait_recv()

                def up_tile(number, carry, core=core):
                    cols = pl.ds(pl.multiple_of(core * units + number * inner, LANES), inner)
                    for top in range(0, width, 256):
                        tile = dot(first_t[top : top + 256, :], slope[:, cols])
                        if core == 1:
                            give(number * width + top, tile)
                        else:
                            take(third + number * width + top, tile)
                    return carry

                lax.fori_loop(low, low + count, up_tile, 0)
                if core == 1:
                    cross(third + low * width, count * width, low * width)
                else:
                    begin_piece(third + low * width, count * width, order)
                poll()
                low += count

        up(1)

        def first_tile(number, carry):
            cols = pl.ds(pl.multiple_of(number * 256, 256), 256)
            wide[:, cols] = (
                gsec[:, cols]
                + dot(slope[:, :units], upw[0, cols, :], NT)
                + dot(slope[:, units:], upw[1, cols, :], NT)
            )
            return carry

        polled_loop(0, width // 256, first_tile, 0)
        up(0)
        def norm_back(number, carry):
            rows = pl.ds(pl.multiple_of(number * block, block), block)
            grad = wide[rows, :]
            normed = normed1[rows, :]
            scaled = grad * row(gain1)
            back = inverse1[rows, 0:1] * (
                scaled
                - jnp.mean(scaled, axis=-1, keepdims=True)
                - normed * jnp.mean(scaled * normed, axis=-1, keepdims=True)
            )
            wide[rows, :] = back
            gmid16[rows, :] = back.astype(BF16)
            return (
                carry[0] + fold8(back),
                carry[1] + fold8(grad * normed),
                carry[2] + fold8(grad),
            )

        totals = lax.fori_loop(0, seq // block, norm_back, (zero, zero, zero))
        both = [jnp.sum(total, axis=0, keepdims=True) for total in totals]
        both += [jnp.sum(total, axis=0, keepdims=True) for total in later]
        vparts[0] = jnp.zeros(vparts.shape[1:], F32)
        vparts[1] = jnp.zeros(vparts.shape[1:], F32)
        for number, line in enumerate(both):
            vparts[0, number : number + 1, :] = line
            vparts[1, number : number + 1, :] = line
        for core in range(2):
            line = jnp.sum(ups[core], axis=0, keepdims=True)
            for side in range(units // width):
                vparts[1 - core, 6 + side : 7 + side, :] = line[:, side * width : (side + 1) * width]
        poll()
        kept.wait()

    def front(upw, downw):
        pl.run_scoped(
            functools.partial(attend_phase, upw, downw),
            pltpu.VMEM((2,) + qkvw_h.shape, BF16),
            pltpu.VMEM((2 * inner, seq), BF16),
            pltpu.VMEM((seq, seq), jnp.int32),
            pltpu.VMEM((seq, seq), jnp.int32),
            pltpu.VMEM((seq, LANES), F32),
            pltpu.VMEM((heads // 2, 8, 2 * LANES), jnp.int32),
            pltpu.VMEM((heads, seq, seq), BF16),
        )
        pl.run_scoped(
            functools.partial(unit_phase, upw, downw),
            pltpu.VMEM((seq, 2 * units), BF16),
            pltpu.VMEM((seq, 2 * units), BF16),
            pltpu.VMEM((seq, width), BF16),
            pltpu.VMEM((width, seq), BF16),
            pltpu.VMEM((seq, width), F32),
            pltpu.VMEM((seq, width), F32),
            pltpu.VMEM((seq, LANES), F32),
            pltpu.VMEM((seq, width), F32),
            pltpu.VMEM((seq, width), BF16),
            pltpu.VMEM((seq, width), BF16),
        )

    pl.run_scoped(
        front,
        pltpu.VMEM((2, width, units), BF16),
        pltpu.VMEM((2, units, width), BF16),
    )

    def pair_phase(spread, gq, gk, gv, kt, dheads_t, dheads, expo, expo_sem):
        def fetch(pair):
            slot = pair % 2 if isinstance(pair, int) else lax.rem(pair, 2)
            return pltpu.make_async_copy(
                expo_h.at[pl.ds(2 * pair, 2)], expo.at[slot], expo_sem.at[slot]
            )

        fetch(0).start()

        full = len(crossed)
        for copy in crossed[full - len(ORDERS["up"]) :]:
            copy().wait_send()
        at = 2 * third
        other = dot(heads_t[inner:, :], gmid16[...])
        for side in range(split):
            give(side * inner, other[:, side * inner : (side + 1) * inner])
        cross(at, split * inner, 0)
        poll()
        for core in range(2):
            tile = dot(outw[core], gmid16[...], NT)
            for head in range(per):
                rows = slice(core * inner + head * size, core * inner + (head + 1) * size)
                part = tile[head * size : (head + 1) * size] * recip[core * per + head, 0:1, :]
                dheads_t[rows, :] = part.astype(BF16)
        dheads[...] = jnp.transpose(dheads_t[...])
        kt[...] = jnp.transpose(k[...])
        own = dot(heads_t[:inner, :], gmid16[...])
        crossed[full]().wait_recv()
        for side in range(split):
            take(at + side * inner, own[:, side * inner : (side + 1) * inner])
        begin_piece(at, split * inner, ORDERS["out"])
        poll()
        first = lax.broadcasted_iota(jnp.int32, (seq, LANES), 1) < size

        def pair_back(pair, carry):
            cols = pl.ds(pl.multiple_of(pair * LANES, LANES), LANES)
            fetch(pair).wait()

            @pl.when(pair + 1 < heads // 2)
            def _():
                fetch(pair + 1).start()

            slot = lax.rem(pair, 2)
            values, queries = v[:, cols], q[:, cols]
            grads, grads_t = dheads[:, cols], dheads_t[cols, :]
            gvs, gks, gqs = [], [], []
            for side in range(2):
                head = 2 * pair + side
                mine = first if side == 0 else jnp.logical_not(first)
                rows = pl.ds(pl.multiple_of(pair * LANES + side * size, size), size)
                shift = jnp.sum(
                    dheads_t[rows, :].astype(F32) * heads_t[rows, :].astype(F32),
                    axis=0,
                    keepdims=True,
                )
                back = dot(jnp.where(mine, values, jnp.zeros_like(values)), grads_t)
                gscore = expo[slot, side].astype(F32) * (back - shift)
                for tile in range(seq // LANES):
                    spread[pl.ds(tile * seq * 16 + head, seq, stride=16), :] = gscore[
                        :, tile * LANES : (tile + 1) * LANES
                    ]
                gscore = gscore.astype(BF16)
                gvs.append(dot(expo[slot, side], grads))
                gks.append(dot(gscore, queries))
                gqs.append(dot(kt[rows, :], gscore) * 0.125)
            gv[:, cols] = jnp.where(first, gvs[0], gvs[1]).astype(BF16)
            gk[:, cols] = jnp.where(first, gks[0], gks[1]).astype(BF16)
            gq[:, cols] = jnp.transpose(jnp.concatenate(gqs, axis=0)).astype(BF16)
            return carry

        polled_loop(0, heads // 2, pair_back, 0)

    def mix_phase(spread, gq, gk, gv, qkvw, tokens_t):
        l_qkvw = [load(qkvw_h, qkvw.at[0]), load(qkvw_o, qkvw.at[1])]
        tokens_t[...] = jnp.transpose(tokens[...])
        full = len(crossed)
        at = 2 * third + split * inner
        kinds = (gq, gk, gv)
        def mix_back(core):
            for kind in range(3):
                if core == 0:
                    crossed[full + kind]().wait_recv()
                for top in range(0, width, 256):
                    tile = dot(
                        tokens_t[top : top + 256, :],
                        kinds[kind][:, core * inner : (core + 1) * inner],
                    )
                    if core == 1:
                        give(split * inner + kind * width + top, tile)
                    else:
                        take(at + kind * width + top, tile)
                if core == 1:
                    cross(at + kind * width, width, split * inner + kind * width)
                else:
                    begin_piece(at + kind * width, width, ORDERS["mix"][kind])
                poll()

        mix_back(1)
        span = length[me]
        columns = 256
        half_range = LANES // 2
        labels = lax.broadcasted_iota(jnp.int32, (half_range, columns), 0).astype(BF16)
        tab_sum = jnp.zeros((64, half_range), F32)
        for start in range(0, seq, columns):
            here = slice(start, start + columns)
            position = lax.broadcasted_iota(jnp.int32, (1, columns), 1) + start
            inside = (position < span).astype(F32)

            def count(number, carry, here=here, start=start, inside=inside):
                for line in range(64):
                    if line % 16 == 0:
                        place = pl.multiple_of(number * 64 + line, 16)
                        index = bucket[pl.ds(place, 16), here].astype(F32)
                        upper = (index >= half_range).astype(F32)
                        index = (index - upper * half_range).astype(BF16)
                        place = pl.multiple_of(place * 16, 256)
                        grads = jnp.concatenate(
                            [
                                spread[pl.ds(tile * seq * 16 + place, 256), :]
                                for tile in range(start // LANES, (start + columns) // LANES)
                            ],
                            axis=1,
                        )
                    turn = line % 16
                    hot = jnp.where(
                        labels == index[turn : turn + 1, :],
                        jnp.ones((), BF16),
                        jnp.zeros((), BF16),
                    )
                    other = jnp.where(number * 64 + line < span, 1.0 - inside, inside)
                    some = grads[16 * turn : 16 * turn + 16]
                    far = some * other
                    both = jnp.concatenate([some - far, far], axis=0)
                    high = both * upper[turn : turn + 1, :]
                    both = jnp.concatenate([both - high, high], axis=0).astype(BF16)
                    carry = carry + dot(both, hot, NT)
                return carry

            if start == 0:
                tab_sum = polled_loop(0, 2, count, tab_sum)
                mix_back(0)
            tab_sum = polled_loop(0 if start else 2, seq // 64, count, tab_sum)

        for core in range(2):
            mine = slice(core * inner, (core + 1) * inner)
            for number, kind in ((0, gq), (1, gv)):
                line = jnp.sum(fold8(kind[:, mine].astype(F32)), axis=0, keepdims=True)
                vparts[1 - core, 8:9, number * inner : (number + 1) * inner] = line
            for part in range(2):
                lines = []
                for upper in range(2):
                    low = upper * 32 + part * 16 + core * per
                    lines.append(tab_sum[low : low + per])
                cols = slice(part * LANES, (part + 1) * LANES)
                vparts[1 - core, 10 : 10 + per, cols] = jnp.concatenate(lines, axis=1)
        Vectors(vparts, vland, small, bits, kit, vs_sem, vr_sem).run(0)
        poll()

        l_qkvw[0].wait()
        l_qkvw[1].wait()

        def token_tile(number, carry):
            cols = pl.ds(pl.multiple_of(number * 256, 256), 256)
            total = wide[:, cols]
            for core in range(2):
                for kind in range(3):
                    total = total + dot(
                        kinds[kind][:, core * inner : (core + 1) * inner],
                        qkvw[core, kind, cols, :],
                        NT,
                    )
            wide[:, cols] = total
            return carry

        polled_loop(0, width // 256, token_tile, 0)

    per = heads // 2
    size = inner // per

    def back(spread, gq, gk, gv):
        pl.run_scoped(
            functools.partial(pair_phase, spread, gq, gk, gv),
            pltpu.VMEM((2 * inner, seq), BF16),
            pltpu.VMEM((2 * inner, seq), BF16),
            pltpu.VMEM((seq, 2 * inner), BF16),
            pltpu.VMEM((2, 2, seq, seq), BF16),
            pltpu.SemaphoreType.DMA((2,)),
        )
        pl.run_scoped(
            functools.partial(mix_phase, spread, gq, gk, gv),
            pltpu.VMEM((2,) + qkvw_h.shape, BF16),
            pltpu.VMEM((width, seq), BF16),
        )

    pl.run_scoped(
        back,
        pltpu.VMEM((seq // LANES * seq * 16, LANES), F32),
        pltpu.VMEM((seq, 2 * inner), BF16),
        pltpu.VMEM((seq, 2 * inner), BF16),
        pltpu.VMEM((seq, 2 * inner), BF16),
    )
    done = store(wide, gtok_h)
    for number in range(polls[0], 1 + max(number for number in plan if number != "tail")):
        run_steps(number)
    run_steps("tail")
    done.wait()
    for piece in kit.pieces:
        piece.finish()
    for copy in crossed[-4:]:
        copy().wait_send()
    for number in range(len(halves)):
        half(number).wait_send()


def layer(plan, bits, operands):
    tokens, qkvw, qvb, tab, outw, upw, upb, downw = operands[:8]
    seq, width = tokens.shape
    inner = qkvw.shape[2]
    units = upw.shape[1]
    heads = 2 * tab.shape[0]
    shape = jax.ShapeDtypeStruct
    here = pl.BlockSpec(memory_space=pltpu.VMEM)
    away = pl.BlockSpec(memory_space=pl.ANY)
    scalar = pl.BlockSpec(memory_space=pltpu.SMEM)
    rows = (3 * width * inner + inner * width + 2 * width * units) // inner
    lands = rows - (rows >> 4) + (bits - 4) * (rows >> 4)
    pieces = len(ORDERS["down"]) + len(ORDERS["up"]) + 4
    cuts = [one for _, one, _ in ORDERS["down"] + ORDERS["up"]]
    cuts += [ORDERS["out"][0]] + [one for one, _ in ORDERS["mix"]]
    leave = sum(3 if axis == "D" else 1 for one in cuts for axis in one)
    more = pieces * (bits - 4)
    return pl.pallas_call(
        functools.partial(layer_kernel, plan, bits),
        out_shape=(
            shape((rows, inner), BF16),
            shape((seq, width), F32),
            shape((seq, width), BF16),
            shape((16, width), F32),
            shape(qkvw.shape, BF16),
            shape(outw.shape, BF16),
            shape(upw.shape, BF16),
            shape(downw.shape, BF16),
            shape((heads, seq, seq), BF16),
        ),
        in_specs=[away] * 10 + [here] * 7 + [scalar],
        out_specs=(away, away, away, here) + (away,) * 5,
        scratch_shapes=[
            pltpu.VMEM((rows, inner), BF16),
            pltpu.VMEM((rows // 3, inner), BF16),
            pltpu.VMEM((rows, inner), BF16),
            pltpu.VMEM((lands, inner), BF16),
            pltpu.VMEM((seq, width), BF16),
            pltpu.VMEM((2,) + qvb.shape, F32),
            pltpu.VMEM((2,) + tab.shape, F32),
            pltpu.VMEM(upb.shape, F32),
            pltpu.VMEM(upb.shape, F32),
            pltpu.VMEM((2, 1, units), F32),
            pltpu.VMEM((2,) + outw.shape, BF16),
            pltpu.VMEM((seq, 2 * inner), BF16),
            pltpu.VMEM((seq, 2 * inner), BF16),
            pltpu.VMEM((seq, 2 * inner), BF16),
            pltpu.VMEM((2 * inner, seq), BF16),
            pltpu.VMEM((heads, 8, seq), F32),
            pltpu.VMEM((seq, seq), BF16),
            pltpu.VMEM((seq, width), F32),
            pltpu.VMEM((seq, width), BF16),
            pltpu.VMEM((seq, width), BF16),
            pltpu.VMEM((2, 8, units), F32),
            pltpu.VMEM((bits + 1, 16, width), F32),
            pltpu.VMEM((bits + 1, 16, width), F32),
            pltpu.SemaphoreType.DMA((24,)),
            pltpu.SemaphoreType.DMA((8,)),
            pltpu.SemaphoreType.DMA((leave + more,)),
            pltpu.SemaphoreType.DMA((2 * leave + more,)),
            pltpu.SemaphoreType.DMA((pieces,)),
            pltpu.SemaphoreType.DMA((pieces,)),
            pltpu.SemaphoreType.DMA((pieces,)),
            pltpu.SemaphoreType.DMA((bits + 1,)),
            pltpu.SemaphoreType.DMA((bits + 1,)),
            pltpu.SemaphoreType.DMA((7,)),
            pltpu.SemaphoreType.DMA((7,)),
        ],
        compiler_params=pltpu.CompilerParams(
            collective_id=0, has_side_effects=True, vmem_limit_bytes=VMEM_LIMIT
        ),
    )(*operands)


def finish_kernel(
    flat_h,
    out_h,
    gtok_h,
    small,
    out_f,
    gtok_f,
    mix_f,
    gqv,
    gtab,
    gout_f,
    goutb,
    gain1,
    shift1,
    up_f,
    gupb,
    down_f,
    gdownb,
    gain2,
    shift2,
    flat,
    mix,
    gout,
    up,
    down,
    gtok,
    out,
    in_sem,
    out_sem,
):
    rows, inner = flat.shape
    units, width = down.shape
    split = width // inner
    third = rows // 3
    copies = []
    tiles = units // 256
    span = 256 * split
    sizes = (
        [span] * tiles + [width] * (units // inner) + [split * inner] + [width] * 3
    )
    loads = []
    at = 0
    for number, size in enumerate(sizes):
        here = pl.ds(at, size)
        loads.append(pltpu.make_async_copy(flat_h.at[here, :], flat.at[here, :], in_sem.at[number]))
        loads[-1].start()
        at += size

    for source, target in ((gtok_h, gtok), (out_h, out)):
        loads.append(pltpu.make_async_copy(source, target, in_sem.at[len(loads)]))
        loads[-1].start()

    def store(source, target):
        copies.append(pltpu.make_async_copy(source, target, out_sem.at[len(copies)]))
        copies[-1].start()

    def wide(start, size):
        return flat[start : start + size, :].astype(F32)

    for tile in range(tiles):
        loads[tile].wait()
        here = slice(tile * 256, tile * 256 + 256)
        for side in range(split):
            down[here, side * inner : (side + 1) * inner] = wide(tile * span + side * 256, 256)
        here = pl.ds(tile * 256, 256)
        store(down.at[here, :], down_f.at[here, :])
    for part in range(units // inner):
        loads[tiles + part].wait()
        cols = pl.ds(part * inner, inner)
        up[:, cols] = wide(third + part * width, width)
        store(up.at[:, cols], up_f.at[:, cols])
    at = 2 * third
    loads[-6].wait()
    for side in range(split):
        gout[:, side * inner : (side + 1) * inner] = wide(at + side * inner, inner)
    store(gout, gout_f)
    at += split * inner
    for kind in range(3):
        loads[kind - 5].wait()
        mix[kind] = wide(at + kind * width, width)
        store(mix.at[kind], mix_f.at[kind])
    loads[-2].wait()
    store(gtok, gtok_f)
    loads[-1].wait()
    store(out, out_f)
    for number, vector in enumerate((goutb, gain1, shift1, gdownb, gain2, shift2)):
        vector[...] = small[number : number + 1, :].reshape(width)
    gupb[...] = jnp.concatenate(
        [small[6 + side : 7 + side, :] for side in range(units // width)], axis=1
    ).reshape(units)
    for kind in range(2):
        gqv[kind : kind + 1, :] = small[8:9, kind * inner : (kind + 1) * inner]
    gtab[...] = small[10 : 10 + gtab.shape[0], : gtab.shape[1]]
    for copy in copies:
        copy.wait()


def finish(flat, small, out, grad_tokens, width, units, heads):
    shape = jax.ShapeDtypeStruct
    here = pl.BlockSpec(memory_space=pltpu.VMEM)
    away = pl.BlockSpec(memory_space=pl.ANY)
    inner = flat.shape[1]
    vector = shape((width,), F32)
    got = pl.pallas_call(
        finish_kernel,
        out_shape=(
            shape(out.shape, BF16),
            shape(grad_tokens.shape, F32),
            shape((3, width, inner), F32),
            shape((2, inner), F32),
            shape((heads, 2 * LANES), F32),
            shape((inner, width), F32),
            vector,
            vector,
            vector,
            shape((width, units), F32),
            shape((units,), F32),
            shape((units, width), F32),
            vector,
            vector,
            vector,
        ),
        in_specs=[away] * 3 + [here],
        out_specs=(away, away, away, here, here, away, here, here, here, away, here, away)
        + (here,) * 3,
        scratch_shapes=[
            pltpu.VMEM(flat.shape, BF16),
            pltpu.VMEM((3, width, inner), F32),
            pltpu.VMEM((inner, width), F32),
            pltpu.VMEM((width, units), F32),
            pltpu.VMEM((units, width), F32),
            pltpu.VMEM(grad_tokens.shape, F32),
            pltpu.VMEM(out.shape, BF16),
            pltpu.SemaphoreType.DMA((units // 256 + units // inner + 6,)),
            pltpu.SemaphoreType.DMA((units // 256 + units // inner + 6,)),
        ],
        compiler_params=pltpu.CompilerParams(vmem_limit_bytes=VMEM_LIMIT),
    )(flat, out, grad_tokens, small)
    got = list(got)
    got[2] = jnp.transpose(got[2], (1, 0, 2))
    got[4] = got[4].T
    return tuple(got)


def order_of_steps(bits):
    pieces = len(ORDERS["down"]) + len(ORDERS["up"]) + 4
    plan = dict(PAUSES)
    known = {step for steps in PAUSES.values() for step in steps} | set(TAIL)
    more = tuple((pieces, step) for step in range(1, bits + 2) if (pieces, step) not in known)
    plan["tail"] = TAIL + more
    return plan


def on_device(
    dp,
    tokens,
    qkv_weight,
    qv_bias,
    rel_table,
    out_weight,
    out_bias,
    norm1_gain,
    norm1_bias,
    up_weight,
    up_bias,
    down_weight,
    down_bias,
    norm2_gain,
    norm2_bias,
    rel_bucket,
    query_len,
    key_mask,
    upstream,
):
    width = tokens.shape[1]
    units = up_weight.shape[1]
    bits = int(math.log2(dp))
    flat, grad_tokens, out, small = layer(
        order_of_steps(bits),
        bits,
        (
            tokens,
            jnp.transpose(qkv_weight, (1, 0, 2)),
            qv_bias,
            rel_table.T,
            out_weight,
            up_weight,
            up_bias,
            down_weight,
            upstream,
            rel_bucket,
            out_bias,
            norm1_gain,
            norm1_bias,
            down_bias,
            norm2_gain,
            norm2_bias,
            key_mask,
            query_len,
        ),
    )[:4]
    return finish(flat, small, out, grad_tokens, width, units, rel_table.shape[1])


def solution(mesh):
    rows = P(("dp", "tensor"), None)
    whole = P()
    in_specs = (
        rows,
        P(None, None, "tensor"),
        P(None, "tensor"),
        P(None, "tensor"),
        P("tensor", None),
        whole,
        whole,
        whole,
        P(None, "tensor"),
        P("tensor"),
        P("tensor", None),
        whole,
        whole,
        whole,
        whole,
        P("dp"),
        P("dp", None),
        rows,
    )
    out_specs = (
        rows,
        rows,
        P(None, None, "tensor"),
        P(None, "tensor"),
        P(None, "tensor"),
        P("tensor", None),
        whole,
        whole,
        whole,
        P(None, "tensor"),
        P("tensor"),
        P("tensor", None),
        whole,
        whole,
        whole,
    )
    return jax.shard_map(
        functools.partial(on_device, mesh.shape["dp"]),
        mesh=mesh,
        in_specs=in_specs,
        out_specs=out_specs,
        check_vma=False,
    )
```

profile of v0, /device:TPU:0, one launch (start us, length us, event | category | flops | bytes accessed | tf_op | source)
XLA Modules:
  0.0 165.1 jit_solution(6329202298182306154)
XLA Ops:
  0.7 153.9 %shard_map.289 = (bf16[9216,384]{1,0:T(8,128)(2,1)}, f32[512,768]{1,0:T(8,128)}, bf16[512,768]{1,0:T(8,128)(2,1)}, f32[16,768]{1,0:T(8,128)}, bf16[3,768,384]{2,...) custom-call(bf16[512,768]{1,0:T(8,128)(2,1)} %tokens_h.1, ...), custom_call_target="tpu_custom_call" | custom-call | tf_op jit(solution)/shard_map/pallas_call | solution.py:1076
  154.5 10.4 %shard_map.290 = (bf16[512,768]{1,0:T(8,128)(2,1)}, f32[512,768]{1,0:T(8,128)}, f32[3,768,384]{2,1,0:T(8,128)}, f32[2,384]{1,0:T(2,128)}, f32[6,256]{1,0:T(8,128...) custom-call(bf16[9216,384]{1,0:T(8,128)(2,1)} %get-tuple-element.34., ...), custom_call_target="tpu_custom_call" | custom-call | tf_op jit(solution)/shard_map/pallas_call | solution.py:1236
where the time goes:
time: 165 us
  Pallas kernels  164 us (99%)
    pallas_call x1, Pallas kernels, layer(): pl.pallas_call(functools.partial(layer_kernel, plan, bits), out_shape=(sh...  154 us
    pallas_call x1, Pallas kernels, finish(): pl.pallas_call(finish_kernel, out_shape=(shape(out.shape, BF16), shape(gr...  10.4 us

commit v1 on v0

--- a/solution.py
+++ b/solution.py
@@ -1194,13 +1194,18 @@
         here = slice(tile * 256, tile * 256 + 256)
         for side in range(split):
             down[here, side * inner : (side + 1) * inner] = wide(tile * span + side * 256, 256)
-        here = pl.ds(tile * 256, 256)
-        store(down.at[here, :], down_f.at[here, :])
-    for part in range(units // inner):
+        if tile % 2:
+            here = pl.ds(tile * 256 - 256, 512)
+            store(down.at[here, :], down_f.at[here, :])
+    parts = units // inner
+    for part in range(parts):
         loads[tiles + part].wait()
-        cols = pl.ds(part * inner, inner)
-        up[:, cols] = wide(third + part * width, width)
-        store(up.at[:, cols], up_f.at[:, cols])
+    for top in range(0, width, 256):
+        for part in range(parts):
+            cols = slice(part * inner, (part + 1) * inner)
+            up[top : top + 256, cols] = wide(third + part * width + top, 256)
+        here = pl.ds(top, 256)
+        store(up.at[here, :], up_f.at[here, :])
     at = 2 * third
     loads[-6].wait()
     for side in range(split):

time: 165 us -> 165 us (level)
  no operation moved by 1% of the time
where the time goes in v1:
time: 165 us
  Pallas kernels  164 us (99%)
    pallas_call x1, Pallas kernels, layer(): pl.pallas_call(functools.partial(layer_kernel, plan, bits), out_shape=(sh...  154 us
    pallas_call x1, Pallas kernels, finish(): pl.pallas_call(finish_kernel, out_shape=(shape(out.shape, BF16), shape(gr...  10.1 us

profile of v1, /device:TPU:0, one launch (start us, length us, event | category | flops | bytes accessed | tf_op | source)
XLA Modules:
  0.0 164.8 jit_solution(2306775779681924877)
XLA Ops:
  0.7 153.9 %shard_map.289 = (bf16[9216,384]{1,0:T(8,128)(2,1)}, f32[512,768]{1,0:T(8,128)}, bf16[512,768]{1,0:T(8,128)(2,1)}, f32[16,768]{1,0:T(8,128)}, bf16[3,768,384]{2,...) custom-call(bf16[512,768]{1,0:T(8,128)(2,1)} %tokens_h.1, ...), custom_call_target="tpu_custom_call" | custom-call | tf_op jit(solution)/shard_map/pallas_call | solution.py:1076
  154.5 10.1 %shard_map.290 = (bf16[512,768]{1,0:T(8,128)(2,1)}, f32[512,768]{1,0:T(8,128)}, f32[3,768,384]{2,1,0:T(8,128)}, f32[2,384]{1,0:T(2,128)}, f32[6,256]{1,0:T(8,128...) custom-call(bf16[9216,384]{1,0:T(8,128)(2,1)} %get-tuple-element.34., ...), custom_call_target="tpu_custom_call" | custom-call | tf_op jit(solution)/shard_map/pallas_call | solution.py:1241
